TPU v7x, 32 devices: a whole 2x2x4 slice. The times are simulated.
32 devices in a mesh: ctx: 8 (over z, core), tp: 4 (over y, x).
Axes of the slice: x: 2, y: 2, z: 4, core: 2. Of those that a mesh axis runs over, the one named last changes fastest.
Arguments:
- query_field: bfloat16 [8192, 4096], P('ctx', 'tp'), may hold values from -6 to 6
- key_field: bfloat16 [8192, 4096], P('ctx', 'tp'), may hold values from -6 to 6
- value_field: bfloat16 [8192, 4096], P('ctx', 'tp'), may hold values from -6 to 6
- upstream: bfloat16 [8192, 4096], P('ctx', 'tp'), may hold values from -6 to 6
- decay_rates: float32 [16, 4096], P(None, 'tp'), may hold values from 6.1035156e-05 to 0.05
- frequencies: float32 [16, 4096], P(None, 'tp'), may hold values from 0 to 1
- residues: float32 [16, 4096], P(None, 'tp'), may hold values from -1.5 to 1.5
- passthrough: float32 [4096], P('tp'), may hold values from 0.5 to 1.5
- norm_gain: float32 [4096], P('tp'), may hold values from 0.5 to 1.5
Outputs:
- output: bfloat16 [8192, 4096], P('ctx', 'tp')
- grad_queries: bfloat16 [8192, 4096], P('ctx', 'tp')
- grad_keys: bfloat16 [8192, 4096], P('ctx', 'tp')
- grad_values: bfloat16 [8192, 4096], P('ctx', 'tp')
- grad_gain: float32 [4096], P('tp')
All inputs are finite; a program needn't handle non-finite values.
Results may differ from a plain program's by a relative error of at most 0.01.
Values may be sent and summed in bfloat16 or wider, within the bound.
A program may use at most 192 MiB of HBM per device.

v0:
```python
import functools

import jax
import jax.numpy as jnp
from jax import lax
from jax.experimental import pallas as pl
from jax.experimental.pallas import tpu as pltpu
from jax.sharding import PartitionSpec as P

D = 4096
EPS = 1e-06
B = 16
LANES = 128
F32 = jnp.float32
BF16 = jnp.bfloat16


def permute_in(x, nat, perm, chunks):
    nat[...] = x
    for b in range(B):
        perm[pl.ds(b * chunks, chunks), :] = nat[pl.ds(b, chunks, stride=B), :]


def chunk_states(perm, powers, states, modes, chunks, forward):
    def step(i, carry):
        total = [[jnp.zeros((chunks, LANES), F32) for _ in range(2)] for _ in range(2)]
        for b in range(B):
            x = perm[pl.ds(b * chunks, chunks), :]
            k = B - b if forward else b + 1
            for j in range(2):
                m = 2 * i + j
                total[j][0] = total[j][0] + powers[m, k : k + 1, :] * x
                total[j][1] = total[j][1] + powers[m, B + 1 + k : B + 2 + k, :] * x
        for j in range(2):
            for part in range(2):
                row = pl.multiple_of((part * modes + 2 * i + j) * chunks, 8)
                states[pl.ds(row, chunks), :] = total[j][part]
        return carry

    lax.fori_loop(0, modes // 2, step, 0)


def scan_chunks(states, first_re, first_im, powers_re, powers_im, out, modes, chunks, forward):
    def step(n, carry):
        re, im = carry
        a = n if forward else chunks - 1 - n
        at_re = pl.ds(a, modes, stride=chunks)
        at_im = pl.ds(modes * chunks + a, modes, stride=chunks)
        own_re = states[at_re, :]
        own_im = states[at_im, :]
        if out is not None:
            out[at_re, :] = re
            out[at_im, :] = im
        return (
            powers_re * re - powers_im * im + own_re,
            powers_re * im + powers_im * re + own_im,
        )

    return lax.fori_loop(0, chunks, step, (first_re, first_im), unroll=4)


def expand(perm, incoming, taps, gains, result, modes, chunks, forward):
    width = 4
    for g in range(B // width):
        rows = [g * width + j for j in range(width)]
        total = [None] * width
        for s in range(B):
            lags = [(t - s if forward else s - t) for t in rows]
            if max(lags) < 0:
                continue
            x = perm[pl.ds(s * chunks, chunks), :]
            for j, lag in enumerate(lags):
                if lag >= 0:
                    term = taps[lag : lag + 1, :] * x
                    total[j] = term if total[j] is None else total[j] + term

        def step(i, carry):
            carry = list(carry)
            for h in range(2):
                m = 2 * i + h
                re = incoming[pl.ds(pl.multiple_of(m * chunks, 8), chunks), :]
                im = incoming[pl.ds(pl.multiple_of((modes + m) * chunks, 8), chunks), :]
                for j, t in enumerate(rows):
                    k = t if forward else B - 1 - t
                    carry[j] = (
                        carry[j] + gains[m, k : k + 1, :] * re + gains[m, B + k : B + k + 1, :] * im
                    )
            return tuple(carry)

        total = lax.fori_loop(0, modes // 2, step, tuple(total))
        for j, t in enumerate(rows):
            result[pl.ds(t, chunks, stride=B), :] = total[j]


def forward_states_kernel(modes, chunks, key, value, powers, jump, states, last, nat, perm):
    field = (key[...].astype(F32) * value[...].astype(F32)).astype(BF16).astype(F32)
    permute_in(field, nat, perm, chunks)
    chunk_states(perm, powers, states, modes, chunks, True)
    zero = jnp.zeros((modes, LANES), F32)
    re, im = scan_chunks(states, zero, zero, jump[0], jump[1], None, modes, chunks, True)
    last[0] = re
    last[1] = im


def forward_kernel(
    modes, chunks, key, value, query, up, gain, states, first, jump, taps, gains,
    conv, squares, inners, nat, perm, incoming,
):
    field = (key[...].astype(F32) * value[...].astype(F32)).astype(BF16).astype(F32)
    permute_in(field, nat, perm, chunks)
    scan_chunks(states, first[0], first[1], jump[0], jump[1], incoming, modes, chunks, True)
    expand(perm, incoming, taps, gains, nat, modes, chunks, True)
    conv_out = nat[...].astype(BF16)
    conv[...] = conv_out
    gated = query[...].astype(F32) * conv_out.astype(F32)

    @pl.when(pl.program_id(0) == 0)
    def _():
        squares[...] = jnp.zeros_like(squares)
        inners[...] = jnp.zeros_like(inners)

    squares[...] += gated * gated
    inners[...] += up[...].astype(F32) * gain[...] * gated


def middle_kernel(
    modes, chunks, query, up, conv, gain, scale, inner, powers, jump,
    output, query_grad, conv_grad, gain_grad, states, last, nat, perm,
):
    q = query[...].astype(F32)
    c = conv[...].astype(F32)
    u = up[...].astype(F32)
    s = scale[...]
    normed = q * c * s
    output[...] = (normed * gain[...]).astype(BF16)
    gain_grad[...] = jnp.sum(u * normed, axis=0, keepdims=True)
    grad_gated = s * (u * gain[...] - normed * inner[...])
    query_grad[...] = (grad_gated * c).astype(BF16)
    w = (grad_gated * q).astype(BF16)
    conv_grad[...] = w
    permute_in(w.astype(F32), nat, perm, chunks)
    chunk_states(perm, powers, states, modes, chunks, False)
    zero = jnp.zeros((modes, LANES), F32)
    re, im = scan_chunks(states, zero, zero, jump[0], jump[1], None, modes, chunks, False)
    last[0] = re
    last[1] = im


def backward_kernel(
    modes, chunks, conv_grad, key, value, states, first, jump, taps, gains,
    key_grad, value_grad, nat, perm, incoming,
):
    permute_in(conv_grad[...].astype(F32), nat, perm, chunks)
    scan_chunks(states, first[0], first[1], jump[0], jump[1], incoming, modes, chunks, False)
    expand(perm, incoming, taps, gains, nat, modes, chunks, False)
    field_grad = nat[...].astype(BF16).astype(F32)
    key_grad[...] = (field_grad * value[...].astype(F32)).astype(BF16)
    value_grad[...] = (field_grad * key[...].astype(F32)).astype(BF16)


def body(query, key, value, up, rates, freqs, residues, passthrough, norm_gain):
    tokens, width = query.shape
    modes = rates.shape[0]
    chunks = tokens // B
    blocks = width // LANES
    groups = lax.axis_size("ctx")
    me = lax.axis_index("ctx")

    def power(n):
        size = jnp.exp(-rates * n)
        return size * jnp.cos(freqs * n), size * jnp.sin(freqs * n)

    steps = jnp.arange(B + 1, dtype=F32)[None, :, None]
    size = jnp.exp(-rates[:, None, :] * steps)
    angle = freqs[:, None, :] * steps
    pow_re, pow_im = size * jnp.cos(angle), size * jnp.sin(angle)
    powers = jnp.concatenate([pow_re, pow_im], axis=1)
    weight = (residues * jnp.sqrt(rates))[:, None, :]
    gains = jnp.concatenate([weight * pow_re[:, :B], -weight * pow_im[:, :B]], axis=1)
    taps = jnp.sum(weight * pow_re[:, :B], axis=0)
    taps = taps.at[0].add(passthrough)
    jump = jnp.stack([pow_re[:, B], pow_im[:, B]])
    gain = norm_gain[None, :]

    def first_state(last, order):
        every = lax.all_gather(last, "ctx", axis=0)
        away = jnp.where(order > 0, order - 1, 0)[:, None, None].astype(F32) * tokens
        on = (order > 0)[:, None, None]
        size = jnp.where(on, jnp.exp(-rates[None] * away), 0.0)
        re, im = size * jnp.cos(freqs[None] * away), size * jnp.sin(freqs[None] * away)
        s_re, s_im = every[:, 0], every[:, 1]
        return jnp.stack(
            [jnp.sum(re * s_re - im * s_im, axis=0), jnp.sum(re * s_im + im * s_re, axis=0)]
        )

    place = jnp.arange(groups)
    tile = pl.BlockSpec((tokens, LANES), lambda i: (0, i))
    fixed = pl.BlockSpec((tokens, LANES), lambda i: (0, 0))
    row = pl.BlockSpec((1, LANES), lambda i: (0, i))
    pow_spec = pl.BlockSpec((modes, 2 * (B + 1), LANES), lambda i: (0, 0, i))
    gains_spec = pl.BlockSpec((modes, 2 * B, LANES), lambda i: (0, 0, i))
    taps_spec = pl.BlockSpec((B, LANES), lambda i: (0, i))
    pair = pl.BlockSpec((2, modes, LANES), lambda i: (0, 0, i))
    states_spec = pl.BlockSpec((2 * modes * chunks, LANES), lambda i: (0, i))
    field_shape = jax.ShapeDtypeStruct((tokens, width), BF16)
    sums_shape = jax.ShapeDtypeStruct((tokens, LANES), F32)
    states_shape = jax.ShapeDtypeStruct((2 * modes * chunks, width), F32)
    pair_shape = jax.ShapeDtypeStruct((2, modes, width), F32)
    scratch = [pltpu.VMEM((tokens, LANES), F32), pltpu.VMEM((tokens, LANES), F32)]
    incoming = pltpu.VMEM((2 * modes * chunks, LANES), F32)
    params = pltpu.CompilerParams(vmem_limit_bytes=48 * 1024 * 1024)

    def call(kernel, ins, outs, shapes, more, *args):
        return pl.pallas_call(
            functools.partial(kernel, modes, chunks),
            grid=(blocks,),
            in_specs=ins,
            out_specs=outs,
            out_shape=shapes,
            scratch_shapes=scratch + more,
            compiler_params=params,
        )(*args)

    states, last = call(
        forward_states_kernel,
        [tile, tile, pow_spec, pair],
        [states_spec, pair],
        [states_shape, pair_shape],
        [],
        key, value, powers, jump,
    )
    first = first_state(last, me - place)
    conv, squares, inners = call(
        forward_kernel,
        [tile, tile, tile, tile, row, states_spec, pair, pair, taps_spec, gains_spec],
        [tile, fixed, fixed],
        [field_shape, sums_shape, sums_shape],
        [incoming],
        key, value, query, up, gain, states, first, jump, taps, gains,
    )
    sums = lax.psum(jnp.stack([jnp.sum(squares, axis=1), jnp.sum(inners, axis=1)]), "tp")
    scale = lax.rsqrt(sums[0] / D + EPS)
    inner = sums[1] * scale / D
    scale_wide = jnp.broadcast_to(scale[:, None], (tokens, LANES))
    inner_wide = jnp.broadcast_to(inner[:, None], (tokens, LANES))
    output, query_grad, conv_grad, gain_part, states, last = call(
        middle_kernel,
        [tile, tile, tile, row, fixed, fixed, pow_spec, pair],
        [tile, tile, tile, row, states_spec, pair],
        [field_shape] * 3 + [jax.ShapeDtypeStruct((1, width), F32), states_shape, pair_shape],
        [],
        query, up, conv, gain, scale_wide, inner_wide, powers, jump,
    )
    gain_grad = lax.psum(gain_part[0], "ctx")
    first = first_state(last, place - me)
    key_grad, value_grad = call(
        backward_kernel,
        [tile, tile, tile, states_spec, pair, pair, taps_spec, gains_spec],
        [tile, tile],
        [field_shape] * 2,
        [incoming],
        conv_grad, key, value, states, first, jump, taps, gains,
    )
    return output, query_grad, key_grad, value_grad, gain_grad


def solution(mesh):
    field = P("ctx", "tp")
    return jax.shard_map(
        body,
        mesh=mesh,
        in_specs=(field,) * 4 + (P(None, "tp"),) * 3 + (P("tp"),) * 2,
        out_specs=(field,) * 4 + (P("tp"),),
        check_vma=False,
    )
```

profile of v0, /device:TPU:0, one launch (start us, length us, event | category | flops | bytes accessed | tf_op | source)
XLA Modules:
  0.0 216.2 jit_solution(4192711247900145158)
XLA Ops:
  7.2 0.0 all-gather.5.cloned.1.call-start
  7.2 0.9 fusion.8
  8.1 6.5 %cosine_multiply_fusion = (f32[16,17,1024]{2,1,0:T(8,128)S(1)}, f32[16,17,1024]{2,1,0:T(8,128)S(1)}) fusion(f32[16,1024]{1,0:T(8,128)} %param.16, f32[16,1024]{1,0:T(8,128)S(1)} %get-tuple-element.53), kind=kLoop, calls=%fused_computation.3 | loop fusion | flops 1114112 | bytes 2359296 | tf_op jit(solution)/shard_map/mul | solution.py:176
  14.7 0.1 slice_bitcast_fusion.4
  14.8 1.9 pad_maximum_fusion.powers
  16.7 0.1 copy-done.7
  16.7 0.8 copy-done.8
  17.5 0.1 pad_maximum_fusion.2
  17.7 0.2 copy-done
  17.9 1.1 copy-done.1
  19.0 20.7 %shard_map.128 = (f32[2048,1024]{1,0:T(8,128)}, f32[2,16,1024]{2,1,0:T(8,128)}) custom-call(bf16[1024,1024]{1,0:T(8,128)(2,1)S(1)} %copy-done, bf16[1024,1024]{1,0:T(8,128)(2,1)S(1)} %copy-done.1, f32[16,34,1024]{2,1,0:T(8,128)} %pad_maximum_fusion.powers, f32[2,16,1024]{2,1,0:T(8,128)S(1)} %copy.21.jump), custom_call_target="tpu_custom_call" | custom-call | tf_op jit(solution)/shard_map/pallas_call | solution.py:214
  39.7 0.0 all-gather.7.cloned.1.call-start
  39.8 2.8 %fusion.9 = (f32[16,1024]{1,0:T(8,128)S(1)}, f32[16,16,1024]{2,1,0:T(8,128)S(1)}, f32[16,16,1024]{2,1,0:T(8,128)}) fusion(f32[16,17,1024]{2,1,0:T(8,128)} %copy-done.7, f32[16,1024]{1,0:T(8,128)S(1)} %get-tuple-element.48, f32[16,17,1024]{2,1,0:T(8,128)} %copy-done.8, f32[16,1024]{1,0:T(8,128)S(1)} %get-tuple-element.47), kind=kLoop, calls=%fused_computation.45 | loop fusion | flops 770048 | bytes 4390912 | tf_op jit(solution)/shard_map/reduce_sum | solution.py:180
  42.6 0.1 scatter-add.4.taps
  42.8 2.8 %pad_maximum_fusion.1.gains = f32[16,32,1024]{2,1,0:T(8,128)} fusion(f32[16,16,1024]{2,1,0:T(8,128)} %get-tuple-element.56, f32[16,16,1024]{2,1,0:T(8,128)S(1)} %get-tuple-element.50), kind=kLoop, calls=%fused_computation.1 | loop fusion | flops 524288 | bytes 4194304 | tf_op jit(solution)/shard_map/concatenate | solution.py:179
  45.6 19.1 %all-gather.5.cloned.1.call-done = f32[16,16,1024]{2,1,0:T(8,128)} async-done(((f32[2,16,1024]{2,1,0:T(8,128)}), f32[16,16,1024]{2,1,0:T(8,128)}) %all-gather.5.cloned.1.call-update) | async-done | bytes 1048592 | tf_op jit(solution)/shard_map/all_gather | solution.py:186
  64.7 3.8 %subtract_reduce_fusion.1 = (f32[16,1024]{1,0:T(8,128)S(1)}, f32[16,1024]{1,0:T(8,128)S(1)}) fusion(f32[8,2,16,1024]{3,2,1,0:T(8,128)} %bitcast.50, f32[16,1024]{1,0:T(8,128)S(1)} %copy-done.9, f32[8]{0:T(128)S(1)} %convert_multiply_fusion.1, f32[16,1024]{1,0:T(8,128)S(1)} %get-tuple-element.53, pred[8]{0:T(512)(128)(4,1)S(1)} %fusion.7), kind=kLoop, calls=%fused_computation.24 | loop fusion | flops 1671168 | bytes 1310760 | tf_op jit(solution)/shard_map/reduce_sum | solution.py:193
  68.5 35.6 %shard_map.129 = (bf16[1024,1024]{1,0:T(8,128)(2,1)S(1)}, f32[1024,128]{1,0:T(8,128)S(1)}, f32[1024,128]{1,0:T(8,128)S(1)}) custom-call(bf16[1024,1024]{1,0:T(8,128)(2,1)S(1)} %copy-done, bf16[1024,1024]{1,0:T(8,128)(2,1)} %value.5, bf16[1024,1024]{1,0:T(8,128)(2,1)} %query.3, bf16[1024,1024]{1,0:T(8,128)(2,1)} %up.3, f32[1,1024]{1,0:T(1,128)S(1)} %bitcast.47, ...), custom_call_target="tpu_custom_call" | custom-call | tf_op jit(solution)/shard_map/pallas_call | solution.py:214
  104.1 1.3 copy-done.3
  105.4 0.2 reduce_sum.67
  105.7 0.2 reduce_sum.66
  105.9 10.2 %psum.14 = f32[2,1024]{1,0:T(2,128)S(1)} all-reduce(f32[2,1024]{1,0:T(2,128)S(1)} %pad_maximum_fusion.5), channel_id=1, replica_groups=mesh['ctx'=8,'tp'=4] {'tp'}, use_global_device_ids=true, to_apply=%region_5.6 | all-reduce | flops 2048 | bytes 16384 | tf_op jit(solution)/shard_map/psum | solution.py:241
  116.1 0.2 broadcast_in_dim.31.inner
  116.3 0.2 broadcast_in_dim.30.scale
  116.5 1.6 copy-done.2
  118.1 28.9 %shard_map.130 = (bf16[1024,1024]{1,0:T(8,128)(2,1)}, bf16[1024,1024]{1,0:T(8,128)(2,1)}, bf16[1024,1024]{1,0:T(8,128)(2,1)S(1)}, f32[1,1024]{1,0:T(1,128)S(1)},...) custom-call(bf16[1024,1024]{1,0:T(8,128)(2,1)S(1)} %copy-done.2, bf16[1024,1024]{1,0:T(8,128)(2,1)} %up.3, ...), custom_call_target="tpu_custom_call" | custom-call | tf_op jit(solution)/shard_map/pallas_call | solution.py:214
  147.0 1.3 copy-done.4
  148.4 14.3 %psum.15 = f32[1024]{0:T(1024)} all-reduce(f32[1024]{0:T(1024)S(1)} %bitcast.49), channel_id=1, replica_groups=mesh['ctx'=8,'tp'=4] {'ctx'}, use_global_device_ids=true, to_apply=%region_8.9 | all-reduce | flops 1024 | bytes 8192 | tf_op jit(solution)/shard_map/psum | solution.py:254
  162.7 5.7 %all-gather.7.cloned.1.call-done = f32[16,16,1024]{2,1,0:T(8,128)} async-done(((f32[2,16,1024]{2,1,0:T(8,128)}), f32[16,16,1024]{2,1,0:T(8,128)}) %all-gather.7.cloned.1.call-update) | async-done | bytes 1048592 | tf_op jit(solution)/shard_map/all_gather | solution.py:186
  168.4 3.8 %subtract_reduce_fusion = (f32[16,1024]{1,0:T(8,128)S(1)}, f32[16,1024]{1,0:T(8,128)S(1)}) fusion(f32[8,2,16,1024]{3,2,1,0:T(8,128)} %bitcast.51, f32[8]{0:T(128)S(1)} %convert_multiply_fusion, f32[16,1024]{1,0:T(8,128)S(1)} %copy-done.9, f32[16,1024]{1,0:T(8,128)S(1)} %get-tuple-element.53, pred[8]{0:T(512)(128)(4,1)S(1)} %fusion.6), kind=kLoop, calls=%fused_computation.21 | loop fusion | flops 1671168 | bytes 1310760 | tf_op jit(solution)/shard_map/reduce_sum | solution.py:193
  172.2 1.6 copy-done.5
  173.8 35.5 %shard_map.131 = (bf16[1024,1024]{1,0:T(8,128)(2,1)}, bf16[1024,1024]{1,0:T(8,128)(2,1)}) custom-call(bf16[1024,1024]{1,0:T(8,128)(2,1)S(1)} %copy-done.5, bf16[1024,1024]{1,0:T(8,128)(2,1)S(1)} %copy-done, bf16[1024,1024]{1,0:T(8,128)(2,1)} %value.5, f32[2048,1024]{1,0:T(8,128)} %get-tuple-element.38.states, f32[2,16,1024]{2,1,0:T(8,128)S(1)} %pad_maximum_fusion.4.first, ...), custom_call_target="tpu_custom_call" | custom-call | tf_op jit(solution)/shard_map/pallas_call | solution.py:214
  (27 shorter events, 0.2 us)
Async XLA Ops:
  7.2 57.5 %all-gather.5.cloned.1.call-start = ((), (), s32[]{:S(2)}) async-start(), calls=%async_computation | async-start | bytes 1179648 | tf_op jit(solution)/shard_map/all_gather | solution.py:186
  14.6 2.1 copy-start.7
  14.7 2.9 %copy-start.8 = (f32[16,17,1024]{2,1,0:T(8,128)}, f32[16,17,1024]{2,1,0:T(8,128)S(1)}, u32[]{:S(2)}) copy-start(f32[16,17,1024]{2,1,0:T(8,128)S(1)} %get-tuple-element.52) | copy-start | bytes 3342340
  14.7 3.2 %copy-start = (bf16[1024,1024]{1,0:T(8,128)(2,1)S(1)}, bf16[1024,1024]{1,0:T(8,128)(2,1)}, u32[]{:S(2)}) copy-start(bf16[1024,1024]{1,0:T(8,128)(2,1)} %key.5) | copy-start | bytes 6291460
  14.8 4.2 %copy-start.1 = (bf16[1024,1024]{1,0:T(8,128)(2,1)S(1)}, bf16[1024,1024]{1,0:T(8,128)(2,1)}, u32[]{:S(2)}) copy-start(bf16[1024,1024]{1,0:T(8,128)(2,1)} %value.5) | copy-start | bytes 6291460
  39.7 128.7 %all-gather.7.cloned.1.call-start = ((), (), s32[]{:S(2)}) async-start(), calls=%async_computation.1 | async-start | bytes 1179648 | tf_op jit(solution)/shard_map/all_gather | solution.py:186
  39.8 2.8 %copy-start.10 = (f32[1024]{0:T(1024)S(1)}, f32[1024]{0:T(1024)}, u32[]{:S(2)}) copy-start(f32[1024]{0:T(1024)} %param.18) | copy-start | bytes 12292
  42.8 21.9 %copy-start.9 = (f32[16,1024]{1,0:T(8,128)S(1)}, f32[16,1024]{1,0:T(8,128)}, u32[]{:S(2)}) copy-start(f32[16,1024]{1,0:T(8,128)} %param.16) | copy-start | bytes 196612
  42.8 25.7 %copy-start.6 = (f32[1024]{0:T(1024)S(1)}, f32[1024]{0:T(1024)}, u32[]{:S(2)}) copy-start(f32[1024]{0:T(1024)} %param.19) | copy-start | bytes 12292
  104.1 1.3 copy-start.3
  116.5 1.6 copy-start.2
  147.0 1.3 copy-start.4
  172.2 1.6 copy-start.5
Sparse Core Ops, SparseCore 0:
  39.8 24.7 all-gather.4
  148.5 19.9 all-gather.6
where the time goes:
time: 217 us; the launch traced here: 216 us
  Pallas kernels  121 us (56%)
  waiting for transfers between devices  24.8 us (11%)
  blocking collectives  24.5 us (11%)
  other arithmetic  23.2 us (11%)
  between operations  14.3 us (7%)
  local copies, waits for them, and re-layouts  8.55 us (4%)
    pallas_call x4, Pallas kernels, call(): pl.pallas_call(functools.partial(kernel, modes, chunks), grid=(blocks,),...  121 us
    all_gather x2, waiting for transfers between devices, first_state(): every = lax.all_gather(last, 'ctx', axis=0)  24.8 us
    psum x1, blocking collectives, body(): gain_grad = lax.psum(gain_part[0], 'ctx')  14.3 us
    psum x1, blocking collectives, body(): lax.psum(jnp.stack([jnp.sum(squares, axis=1), jnp.sum(inners, axis=1)]),...  10.2 us
    unnamed x22, local copies, waits for them, and re-layouts  7.95 us
    reduce_sum x2, other arithmetic, first_state(): jnp.sum(re * s_re - im * s_im, axis=0)  7.59 us
    mul x1, other arithmetic, body(): pow_re, pow_im = (size * jnp.cos(angle), size * jnp.sin(angle))  6.52 us
  transfers between devices with their start and end apart: 2, of which 2 were waited for; matrix products, arithmetic and copies ran while one was open for 3% of the time, Pallas kernels for 0%

commit v1 on v0

v1 whole, which is shorter than its diff:
```python
import functools

import jax
import jax.numpy as jnp
from jax import lax
from jax.experimental import pallas as pl
from jax.experimental.pallas import tpu as pltpu
from jax.sharding import PartitionSpec as P

D = 4096
EPS = 1e-06
B = 16
LANES = 128
SEGMENTS = 8
F32 = jnp.float32
BF16 = jnp.bfloat16


def token_rows(x, nat, perm, chunks):
    length = chunks * B
    for s in range(SEGMENTS):
        nat[pl.ds(s * (length + 8), length), :] = x[s * length : (s + 1) * length]
    for b in range(B):
        for a in range(chunks):
            perm[pl.ds((b * chunks + a) * SEGMENTS, SEGMENTS), :] = nat[
                pl.ds(a * B + b, SEGMENTS, stride=length + 8), :
            ]


def token_order(nat, chunks):
    length = chunks * B
    return jnp.concatenate(
        [nat[pl.ds(s * (length + 8), length), :] for s in range(SEGMENTS)], axis=0
    )


def product(a, b):
    return a[0] * b[0] - a[1] * b[1], a[0] * b[1] + a[1] * b[0]


def build_powers(root, powers, chunks):
    one = (root[0], root[1])
    powers[0] = jnp.ones_like(one[0])
    powers[B + 1] = jnp.zeros_like(one[0])
    now = one
    for b in range(1, B + 1):
        powers[b] = now[0]
        powers[B + 1 + b] = now[1]
        if b < B:
            now = product(now, one)
    far, count = None, chunks
    while count:
        if count & 1:
            far = now if far is None else product(far, now)
        count >>= 1
        if count:
            now = product(now, now)
    return far


def build_taps(powers, weight, skip, taps):
    for b in range(B):
        row = jnp.sum(weight[...] * powers[b], axis=0, keepdims=True)
        taps[b : b + 1, :] = row + skip[...] if b == 0 else row


def at(modes, part, m, per):
    return pl.multiple_of((part * modes + m) * per, 8)


def chunk_states(perm, powers, states, ends, modes, chunks, forward):
    count = chunks * SEGMENTS

    def step(i, carry):
        total = [[jnp.zeros((count, LANES), F32) for _ in range(2)] for _ in range(2)]
        for b in range(B):
            x = perm[pl.ds(b * count, count), :]
            k = B - b if forward else b + 1
            for j in range(2):
                m = 2 * i + j
                total[j][0] = total[j][0] + powers[k, pl.ds(m, 1), :] * x
                total[j][1] = total[j][1] + powers[B + 1 + k, pl.ds(m, 1), :] * x
        for j in range(2):
            m = 2 * i + j
            jump = (powers[B, pl.ds(m, 1), :], powers[2 * B + 1, pl.ds(m, 1), :])
            sums = None
            for a in range(chunks) if forward else reversed(range(chunks)):
                own = [total[j][p][a * SEGMENTS : (a + 1) * SEGMENTS] for p in range(2)]
                if sums is not None:
                    moved = product(jump, sums)
                    own = [own[0] + moved[0], own[1] + moved[1]]
                sums = own
            for part in range(2):
                states[pl.ds(at(modes, part, m, count), count), :] = total[j][part]
                ends[pl.ds(at(modes, part, m, SEGMENTS), SEGMENTS), :] = sums[part]
        return carry

    lax.fori_loop(0, modes // 2, step, 0)


def scan_segments(ends, now, far, out, modes, forward):
    for s in range(SEGMENTS) if forward else reversed(range(SEGMENTS)):
        rows = [pl.ds(part * modes * SEGMENTS + s, modes, stride=SEGMENTS) for part in range(2)]
        own = (ends[rows[0], :], ends[rows[1], :])
        if out is not None:
            out[rows[0], :] = now[0]
            out[rows[1], :] = now[1]
        moved = product(far, now)
        now = (moved[0] + own[0], moved[1] + own[1])
    return now


def scan_chunks(states, first, powers, weight, incoming, modes, chunks, forward):
    count = chunks * SEGMENTS

    def step(m, carry):
        jump = (powers[B, pl.ds(m, 1), :], powers[2 * B + 1, pl.ds(m, 1), :])
        scale = weight[pl.ds(m, 1), :]
        now = [first[pl.ds(at(modes, p, m, SEGMENTS), SEGMENTS), :] for p in range(2)]
        for a in range(chunks) if forward else reversed(range(chunks)):
            moved = product(jump, now)
            for p in range(2):
                rows = pl.ds(at(modes, p, m, count) + a * SEGMENTS, SEGMENTS)
                incoming[rows, :] = scale * now[p]
                now[p] = moved[p] + states[rows, :]
        return carry

    lax.fori_loop(0, modes, step, 0, unroll=2)


def expand(perm, incoming, taps, powers, nat, modes, chunks, forward):
    width = 8
    count = chunks * SEGMENTS
    pitch = chunks * B + 8
    part_rows = 2 * SEGMENTS

    for g in range(B // width):
        rows = [g * width + j for j in range(width)]

        def part(h, carry):
            base = pl.multiple_of(h * part_rows, part_rows)
            total = [None] * width
            for s in range(B):
                lags = [(t - s if forward else s - t) for t in rows]
                if max(lags) < 0:
                    continue
                x = perm[pl.ds(s * count + base, part_rows), :]
                for j, lag in enumerate(lags):
                    if lag >= 0:
                        term = taps[lag : lag + 1, :] * x
                        total[j] = term if total[j] is None else total[j] + term

            def step(i, sums):
                sums = list(sums)
                for n in range(4):
                    m = 4 * i + n
                    re = incoming[pl.ds(at(modes, 0, m, count) + base, part_rows), :]
                    im = incoming[pl.ds(at(modes, 1, m, count) + base, part_rows), :]
                    for j, t in enumerate(rows):
                        k = t if forward else B - 1 - t
                        sums[j] = (
                            sums[j]
                            + powers[k, pl.ds(m, 1), :] * re
                            - powers[B + 1 + k, pl.ds(m, 1), :] * im
                        )
                return tuple(sums)

            total = lax.fori_loop(0, modes // 4, step, tuple(total))
            for j, t in enumerate(rows):
                for e in range(2):
                    nat[pl.ds((2 * h + e) * B + t, SEGMENTS, stride=pitch), :] = total[j][
                        e * SEGMENTS : (e + 1) * SEGMENTS
                    ]
            return carry

        lax.fori_loop(0, chunks // 2, part, 0)


def forward_states_kernel(
    modes, chunks, key, value, root, states, ends, last, nat, perm, powers
):
    far = build_powers(root, powers, chunks)
    field = (key[...].astype(F32) * value[...].astype(F32)).astype(BF16).astype(F32)
    token_rows(field, nat, perm, chunks)
    chunk_states(perm, powers, states, ends, modes, chunks, True)
    zero = jnp.zeros((modes, LANES), F32)
    total = scan_segments(ends, (zero, zero), far, None, modes, True)
    last[0:modes, :] = total[0]
    last[modes:, :] = total[1]


def forward_kernel(
    modes, chunks, key, value, query, up, gain, states, ends, first, root, weight, skip,
    conv, squares, inners, nat, perm, powers, incoming, taps, starts,
):
    far = build_powers(root, powers, chunks)
    build_taps(powers, weight, skip, taps)
    field = (key[...].astype(F32) * value[...].astype(F32)).astype(BF16).astype(F32)
    token_rows(field, nat, perm, chunks)
    scan_segments(ends, (first[0], first[1]), far, starts, modes, True)
    scan_chunks(states, starts, powers, weight, incoming, modes, chunks, True)
    expand(perm, incoming, taps, powers, nat, modes, chunks, True)
    conv_out = token_order(nat, chunks).astype(BF16)
    conv[...] = conv_out
    gated = query[...].astype(F32) * conv_out.astype(F32)

    @pl.when(pl.program_id(0) == 0)
    def _():
        squares[...] = jnp.zeros_like(squares)
        inners[...] = jnp.zeros_like(inners)

    squares[...] += gated * gated
    inners[...] += up[...].astype(F32) * gain[...] * gated


def middle_kernel(
    modes, chunks, query, up, conv, gain, scale, inner, root,
    output, query_grad, conv_grad, states, ends, last, nat, perm, powers,
):
    q = query[...].astype(F32)
    c = conv[...].astype(F32)
    u = up[...].astype(F32)
    s = scale[...]
    normed = q * c * s
    output[...] = (normed * gain[...]).astype(BF16)
    gain_grad = jnp.sum(u * normed, axis=0, keepdims=True)
    grad_gated = s * (u * gain[...] - normed * inner[...])
    query_grad[...] = (grad_gated * c).astype(BF16)
    w = (grad_gated * q).astype(BF16)
    conv_grad[...] = w
    far = build_powers(root, powers, chunks)
    token_rows(w.astype(F32), nat, perm, chunks)
    chunk_states(perm, powers, states, ends, modes, chunks, False)
    zero = jnp.zeros((modes, LANES), F32)
    total = scan_segments(ends, (zero, zero), far, None, modes, False)
    last[0:modes, :] = total[0]
    last[modes : 2 * modes, :] = total[1]
    last[2 * modes :, :] = jnp.broadcast_to(gain_grad, (8, LANES))


def backward_kernel(
    modes, chunks, conv_grad, key, value, states, ends, first, root, weight, skip,
    key_grad, value_grad, nat, perm, powers, incoming, taps, starts,
):
    far = build_powers(root, powers, chunks)
    build_taps(powers, weight, skip, taps)
    token_rows(conv_grad[...].astype(F32), nat, perm, chunks)
    scan_segments(ends, (first[0], first[1]), far, starts, modes, False)
    scan_chunks(states, starts, powers, weight, incoming, modes, chunks, False)
    expand(perm, incoming, taps, powers, nat, modes, chunks, False)
    field_grad = token_order(nat, chunks).astype(BF16).astype(F32)
    key_grad[...] = (field_grad * value[...].astype(F32)).astype(BF16)
    value_grad[...] = (field_grad * key[...].astype(F32)).astype(BF16)


def body(query, key, value, up, rates, freqs, residues, passthrough, norm_gain):
    tokens, width = query.shape
    modes = rates.shape[0]
    chunks = tokens // (B * SEGMENTS)
    blocks = width // LANES
    groups = lax.axis_size("ctx")
    me = lax.axis_index("ctx")
    size = jnp.exp(-rates)
    root = jnp.stack([size * jnp.cos(freqs), size * jnp.sin(freqs)])
    weight = residues * jnp.sqrt(rates)
    skip = passthrough[None, :]
    gain = norm_gain[None, :]

    def first_state(every, order):
        away = jnp.where(order > 0, order - 1, 0)[:, None, None].astype(F32) * tokens
        on = (order > 0)[:, None, None]
        size = jnp.where(on, jnp.exp(-rates[None] * away), 0.0)
        re, im = size * jnp.cos(freqs[None] * away), size * jnp.sin(freqs[None] * away)
        s_re, s_im = every[:, :modes], every[:, modes : 2 * modes]
        return jnp.stack(
            [jnp.sum(re * s_re - im * s_im, axis=0), jnp.sum(re * s_im + im * s_re, axis=0)]
        )

    place = jnp.arange(groups)

    def columns(*rows):
        return pl.BlockSpec(rows + (LANES,), lambda i: (0,) * len(rows) + (i,))

    tile = columns(tokens)
    fixed = pl.BlockSpec((tokens, LANES), lambda i: (0, 0))
    row = columns(1)
    pair = columns(2, modes)
    mode = columns(modes)
    states_spec = columns(2 * modes * chunks * SEGMENTS)
    ends_spec = columns(2 * modes * SEGMENTS)
    field_shape = jax.ShapeDtypeStruct((tokens, width), BF16)
    sums_shape = jax.ShapeDtypeStruct((tokens, LANES), F32)

    def wide(rows):
        return jax.ShapeDtypeStruct((rows, width), F32)

    states_shape = wide(2 * modes * chunks * SEGMENTS)
    ends_shape = wide(2 * modes * SEGMENTS)
    scratch = [
        pltpu.VMEM((tokens + 8 * SEGMENTS, LANES), F32),
        pltpu.VMEM((tokens, LANES), F32),
        pltpu.VMEM((2 * (B + 1), modes, LANES), F32),
    ]
    more = [
        pltpu.VMEM((2 * modes * chunks * SEGMENTS, LANES), F32),
        pltpu.VMEM((B, LANES), F32),
        pltpu.VMEM((2 * modes * SEGMENTS, LANES), F32),
    ]
    params = pltpu.CompilerParams(vmem_limit_bytes=56 * 1024 * 1024)

    def call(kernel, ins, outs, shapes, more, *args):
        return pl.pallas_call(
            functools.partial(kernel, modes, chunks),
            grid=(blocks,),
            in_specs=ins,
            out_specs=outs,
            out_shape=shapes,
            scratch_shapes=scratch + more,
            compiler_params=params,
        )(*args)

    states, ends, last = call(
        forward_states_kernel,
        [tile, tile, pair],
        [states_spec, ends_spec, columns(2 * modes)],
        [states_shape, ends_shape, wide(2 * modes)],
        [],
        key, value, root,
    )
    first = first_state(lax.all_gather(last, "ctx", axis=0), me - place)
    conv, squares, inners = call(
        forward_kernel,
        [tile, tile, tile, tile, row, states_spec, ends_spec, pair, pair, mode, row],
        [tile, fixed, fixed],
        [field_shape, sums_shape, sums_shape],
        more,
        key, value, query, up, gain, states, ends, first, root, weight, skip,
    )
    sums = lax.psum(jnp.stack([jnp.sum(squares, axis=1), jnp.sum(inners, axis=1)]), "tp")
    scale = lax.rsqrt(sums[0] / D + EPS)
    inner = sums[1] * scale / D
    scale_wide = jnp.broadcast_to(scale[:, None], (tokens, LANES))
    inner_wide = jnp.broadcast_to(inner[:, None], (tokens, LANES))
    output, query_grad, conv_grad, states, ends, last = call(
        middle_kernel,
        [tile, tile, tile, row, fixed, fixed, pair],
        [tile, tile, tile, states_spec, ends_spec, columns(2 * modes + 8)],
        [field_shape] * 3 + [states_shape, ends_shape, wide(2 * modes + 8)],
        [],
        query, up, conv, gain, scale_wide, inner_wide, root,
    )
    every = lax.all_gather(last[: 2 * modes + 1], "ctx", axis=0)
    gain_grad = jnp.sum(every[:, 2 * modes], axis=0)
    first = first_state(every, place - me)
    key_grad, value_grad = call(
        backward_kernel,
        [tile, tile, tile, states_spec, ends_spec, pair, pair, mode, row],
        [tile, tile],
        [field_shape] * 2,
        more,
        conv_grad, key, value, states, ends, first, root, weight, skip,
    )
    return output, query_grad, key_grad, value_grad, gain_grad


def solution(mesh):
    field = P("ctx", "tp")
    return jax.shard_map(
        body,
        mesh=mesh,
        in_specs=(field,) * 4 + (P(None, "tp"),) * 3 + (P("tp"),) * 2,
        out_specs=(field,) * 4 + (P("tp"),),
        check_vma=False,
    )
```

time: 217 us -> 169 us (0.78)
  Pallas kernels: 121 us -> 78.7 us
  waiting for transfers between devices: 24.8 us -> 46.3 us
  blocking collectives: 24.5 us -> 9.99 us
  other arithmetic: 23.2 us -> 15.5 us
  local copies, waits for them, and re-layouts: 8.55 us -> 3.62 us
    pallas_call x4, Pallas kernels: 121 us -> 78.7 us  [call(): pl.pallas_call(functools.partial(kernel, modes, chunks), grid=(blocks,),...]
    all_gather x2, waiting for transfers between devices: 24.8 us -> 46.3 us  [the longest x1 24.9 us: body(): first = first_state(lax.all_gather(last, 'ctx', axis=0), me - place)]
    psum x1 -> x0, blocking collectives: 14.3 us -> none  [body(): gain_grad = lax.psum(gain_part[0], 'ctx')]
    mul x1 -> x0, other arithmetic: 6.52 us -> none  [body(): pow_re, pow_im = (size * jnp.cos(angle), size * jnp.sin(angle))]
    unnamed x22 -> x3, local copies, waits for them, and re-layouts: 7.95 us -> 1.6 us
    concatenate x2 -> x0, other arithmetic: 4.73 us -> none  [the longest x1 2.82 us: body(): jnp.concatenate([weight * pow_re[:, :B], -weight * pow_im[:, :B]], axis=1)]
    another operation x1 -> x2, other arithmetic: 0.12 us -> 2.41 us  [body(): root = jnp.stack([size * jnp.cos(freqs), size * jnp.sin(freqs)])]
  transfers between devices with their start and end apart: 2 -> 2, of which waited for: 2 -> 2; matrix products, arithmetic and copies ran while one was open for 3% -> 0% of each run, Pallas kernels for 0% -> 0%
where the time goes in v1:
time: 169 us; the launch traced here: 168 us
  Pallas kernels  78.7 us (47%)
  waiting for transfers between devices  46.3 us (27%)
  other arithmetic  15.5 us (9%)
  between operations  14.1 us (8%)
  blocking collectives  9.99 us (6%)
  local copies, waits for them, and re-layouts  3.62 us (2%)
    pallas_call x4, Pallas kernels, call(): pl.pallas_call(functools.partial(kernel, modes, chunks), grid=(blocks,),...  78.7 us
    all_gather x1, waiting for transfers between devices, body(): first = first_state(lax.all_gather(last, 'ctx', axis=0), me - place)  24.9 us
    all_gather x1, waiting for transfers between devices, body(): every = lax.all_gather(last[:2 * modes + 1], 'ctx', axis=0)  21.4 us
    psum x1, blocking collectives, body(): lax.psum(jnp.stack([jnp.sum(squares, axis=1), jnp.sum(inners, axis=1)]),...  9.99 us
    reduce_sum x2, other arithmetic, first_state(): jnp.sum(re * s_re - im * s_im, axis=0)  7.6 us
  transfers between devices with their start and end apart: 2, of which 2 were waited for; matrix products, arithmetic and copies ran while one was open for 0% of the time, Pallas kernels for 0%

profile of v1, /device:TPU:0, one launch (start us, length us, event | category | flops | bytes accessed | tf_op | source)
XLA Modules:
  0.0 168.3 jit_solution(18410632705271018842)
XLA Ops:
  7.2 0.0 all-gather.6.cloned.1.call-start
  7.2 1.8 %multiply_bitcast_fusion.1 = (f32[1,16,1024]{2,1,0:T(8,128)S(1)}, f32[1,16,1024]{2,1,0:T(8,128)S(1)}, f32[16,1024]{1,0:T(8,128)}, f32[16,1024]{1,0:T(8,128)S(1)}) fusion(f32[16,1024]{1,0:T(8,128)} %param.14, f32[16,1024]{1,0:T(8,128)} %param.13, f32[16,1024]{1,0:T(8,128)} %param.15), kind=kLoop, calls=%fused_computation.20 | loop fusion | flops 65536 | bytes 458752 | tf_op jit(solution)/shard_map/stack | solution.py:264
  9.0 0.6 pad_maximum_fusion.root
  9.6 0.0 copy-start
  9.6 16.0 %shard_map.128 = (f32[2048,1024]{1,0:T(8,128)}, f32[256,1024]{1,0:T(8,128)}, f32[32,1024]{1,0:T(8,128)}) custom-call(bf16[1024,1024]{1,0:T(8,128)(2,1)} %key.5, bf16[1024,1024]{1,0:T(8,128)(2,1)} %value.5, f32[2,16,1024]{2,1,0:T(8,128)} %pad_maximum_fusion.root), custom_call_target="tpu_custom_call" | custom-call | tf_op jit(solution)/shard_map/pallas_call | solution.py:312
  25.6 0.0 all-gather.6.cloned.1.call-update
  25.7 0.0 all-gather.8.cloned.1.call-start
  25.7 24.9 %all-gather.6.cloned.1.call-done = f32[256,1024]{1,0:T(8,128)} async-done(((f32[32,1024]{1,0:T(8,128)}), f32[256,1024]{1,0:T(8,128)}) %all-gather.6.cloned.1.call-update) | async-done | bytes 1048592 | tf_op jit(solution)/shard_map/all_gather | solution.py:330
  50.6 0.0 copy-done
  50.6 3.8 %subtract_reduce_fusion.1 = (f32[16,1024]{1,0:T(8,128)S(1)}, f32[16,1024]{1,0:T(8,128)S(1)}) fusion(f32[8,32,1024]{2,1,0:T(8,128)} %bitcast.17, f32[16,1024]{1,0:T(8,128)S(1)} %copy-done, f32[8]{0:T(128)S(1)} %convert_multiply_fusion.1, f32[16,1024]{1,0:T(8,128)S(1)} %get-tuple-element.40, pred[8]{0:T(512)(128)(4,1)S(1)} %fusion.7), kind=kLoop, calls=%fused_computation.12 | loop fusion | flops 1671168 | bytes 1310760 | tf_op jit(solution)/shard_map/reduce_sum | solution.py:276
  54.4 0.7 pad_maximum_fusion.1.first
  55.1 21.8 %shard_map.129 = (bf16[1024,1024]{1,0:T(8,128)(2,1)}, f32[1024,128]{1,0:T(8,128)}, f32[1024,128]{1,0:T(8,128)}) custom-call(bf16[1024,1024]{1,0:T(8,128)(2,1)} %key.5, bf16[1024,1024]{1,0:T(8,128)(2,1)} %value.5, bf16[1024,1024]{1,0:T(8,128)(2,1)} %query.3, bf16[1024,1024]{1,0:T(8,128)(2,1)} %up.3, f32[1,1024]{1,0:T(1,128)} %bitcast.27, ...), custom_call_target="tpu_custom_call" | custom-call | tf_op jit(solution)/shard_map/pallas_call | solution.py:312
  76.9 1.2 reduce_sum.65
  78.1 1.2 reduce_sum.66
  79.4 10.0 %psum.7 = f32[2,1024]{1,0:T(2,128)S(1)} all-reduce(f32[2,1024]{1,0:T(2,128)S(1)} %pad_maximum_fusion.3), channel_id=1, replica_groups=mesh['ctx'=8,'tp'=4] {'tp'}, use_global_device_ids=true, to_apply=%region_4.5 | all-reduce | flops 2048 | bytes 16384 | tf_op jit(solution)/shard_map/psum | solution.py:339
  89.4 1.0 broadcast_in_dim.53.scale
  90.4 1.0 broadcast_in_dim.54.inner
  91.4 20.8 %shard_map.130 = (bf16[1024,1024]{1,0:T(8,128)(2,1)}, bf16[1024,1024]{1,0:T(8,128)(2,1)}, bf16[1024,1024]{1,0:T(8,128)(2,1)}, f32[2048,1024]{1,0:T(8,128)}, f32[256,1024]{1,0:T(8,128)}, /*index=5*/f32[40,1024]{1,0:T(8,128)}) custom-call(bf16[1024,1024]{1,0:T(8,128)(2,1)} %query.3, bf16[1024,1024]{1,0:T(8,128)(2,1)} %up.3, ...), custom_call_target="tpu_custom_call" | custom-call | tf_op jit(solution)/shard_map/pallas_call | solution.py:312
  112.3 1.6 slice_bitcast_fusion
  113.9 0.0 all-gather.8.cloned.1.call-update
  113.9 21.4 %all-gather.8.cloned.1.call-done = f32[8,33,1024]{2,1,0:T(8,128)} async-done(((f32[1,33,1024]{2,1,0:T(8,128)}), f32[8,33,1024]{2,1,0:T(8,128)}) %all-gather.8.cloned.1.call-update) | async-done | bytes 1081360 | tf_op jit(solution)/shard_map/all_gather | solution.py:352
  135.3 3.8 %subtract_reduce_fusion = (f32[16,1024]{1,0:T(8,128)S(1)}, f32[16,1024]{1,0:T(8,128)S(1)}) fusion(f32[8,33,1024]{2,1,0:T(8,128)} %all-gather.8.cloned.1.call-done, f32[8]{0:T(128)S(1)} %convert_multiply_fusion, f32[16,1024]{1,0:T(8,128)S(1)} %copy-done, f32[16,1024]{1,0:T(8,128)S(1)} %get-tuple-element.40, pred[8]{0:T(512)(128)(4,1)S(1)} %fusion.6), kind=kLoop, calls=%fused_computation.9 | loop fusion | flops 1671168 | bytes 1310760 | tf_op jit(solution)/shard_map/reduce_sum | solution.py:276
  139.1 0.7 pad_maximum_fusion.2.first
  139.8 20.1 %shard_map.131 = (bf16[1024,1024]{1,0:T(8,128)(2,1)}, bf16[1024,1024]{1,0:T(8,128)(2,1)}) custom-call(bf16[1024,1024]{1,0:T(8,128)(2,1)} %get-tuple-element.27.conv_grad, bf16[1024,1024]{1,0:T(8,128)(2,1)} %key.5, bf16[1024,1024]{1,0:T(8,128)(2,1)} %value.5, f32[2048,1024]{1,0:T(8,128)} %get-tuple-element.28.states, f32[256,1024]{1,0:T(8,128)} %get-tuple-element.29.ends, ...), custom_call_target="tpu_custom_call" | custom-call | tf_op jit(solution)/shard_map/pallas_call | solution.py:312
  159.9 1.6 slice_reduce_fusion
  (7 shorter events, 0.1 us)
Async XLA Ops:
  7.2 43.5 %all-gather.6.cloned.1.call-start = ((), (), s32[]{:S(2)}) async-start(), calls=%async_computation | async-start | bytes 1179648 | tf_op jit(solution)/shard_map/all_gather | solution.py:330
  9.6 41.0 %copy-start = (f32[16,1024]{1,0:T(8,128)S(1)}, f32[16,1024]{1,0:T(8,128)}, u32[]{:S(2)}) copy-start(f32[16,1024]{1,0:T(8,128)} %param.14) | copy-start | bytes 196612
  25.7 109.6 %all-gather.8.cloned.1.call-start = ((), (), s32[]{:S(2)}) async-start(), calls=%async_computation.1 | async-start | bytes 1474560 | tf_op jit(solution)/shard_map/all_gather | solution.py:352
Sparse Core Ops, SparseCore 0:
  25.8 24.7 all-gather.5
  114.0 21.2 all-gather.7

commit v2 on v1

--- a/solution.py
+++ b/solution.py
@@ -185,8 +185,8 @@
     chunk_states(perm, powers, states, ends, modes, chunks, True)
     zero = jnp.zeros((modes, LANES), F32)
     total = scan_segments(ends, (zero, zero), far, None, modes, True)
-    last[0:modes, :] = total[0]
-    last[modes:, :] = total[1]
+    last[0, 0:modes, :] = total[0]
+    last[0, modes:, :] = total[1]
 
 
 def forward_kernel(
@@ -197,7 +197,7 @@
     build_taps(powers, weight, skip, taps)
     field = (key[...].astype(F32) * value[...].astype(F32)).astype(BF16).astype(F32)
     token_rows(field, nat, perm, chunks)
-    scan_segments(ends, (first[0], first[1]), far, starts, modes, True)
+    scan_segments(ends, (first[0, 0:modes, :], first[0, modes : 2 * modes, :]), far, starts, modes, True)
     scan_chunks(states, starts, powers, weight, incoming, modes, chunks, True)
     expand(perm, incoming, taps, powers, nat, modes, chunks, True)
     conv_out = token_order(nat, chunks).astype(BF16)
@@ -233,9 +233,9 @@
     chunk_states(perm, powers, states, ends, modes, chunks, False)
     zero = jnp.zeros((modes, LANES), F32)
     total = scan_segments(ends, (zero, zero), far, None, modes, False)
-    last[0:modes, :] = total[0]
-    last[modes : 2 * modes, :] = total[1]
-    last[2 * modes :, :] = jnp.broadcast_to(gain_grad, (8, LANES))
+    last[0, 0:modes, :] = total[0]
+    last[0, modes : 2 * modes, :] = total[1]
+    last[0, 2 * modes :, :] = jnp.broadcast_to(gain_grad, (16, LANES))
 
 
 def backward_kernel(
@@ -245,12 +245,134 @@
     far = build_powers(root, powers, chunks)
     build_taps(powers, weight, skip, taps)
     token_rows(conv_grad[...].astype(F32), nat, perm, chunks)
-    scan_segments(ends, (first[0], first[1]), far, starts, modes, False)
+    scan_segments(ends, (first[0, 0:modes, :], first[0, modes : 2 * modes, :]), far, starts, modes, False)
     scan_chunks(states, starts, powers, weight, incoming, modes, chunks, False)
     expand(perm, incoming, taps, powers, nat, modes, chunks, False)
     field_grad = token_order(nat, chunks).astype(BF16).astype(F32)
     key_grad[...] = (field_grad * value[...].astype(F32)).astype(BF16)
     value_grad[...] = (field_grad * key[...].astype(F32)).astype(BF16)
+
+
+def remote(source, target, send, receive, place):
+    return pltpu.make_async_remote_copy(
+        src_ref=source,
+        dst_ref=target,
+        send_sem=send,
+        recv_sem=receive,
+        device_id=place,
+        device_id_type=pl.DeviceIdType.MESH,
+    )
+
+
+def turn(jump, state, modes):
+    return product((jump[:modes], jump[modes:]), (state[:modes], state[modes : 2 * modes]))
+
+
+def exchange_kernel(
+    modes, groups, forward, last, jump, first, sibling_last, slots, own, other, sends, receives
+):
+    pairs = groups // 2
+    me = lax.axis_index("ctx")
+    side = lax.rem(me, 2)
+    pair = me // 2
+    sibling = me + 1 - 2 * side
+    barrier = pltpu.get_barrier_semaphore()
+    pl.semaphore_signal(
+        barrier, inc=1, device_id={"ctx": sibling}, device_id_type=pl.DeviceIdType.MESH
+    )
+    for off in range(1, pairs):
+        to = lax.rem(pair + off, pairs) * 2 + side
+        pl.semaphore_signal(
+            barrier, inc=1, device_id={"ctx": to}, device_id_type=pl.DeviceIdType.MESH
+        )
+    pl.semaphore_wait(barrier, pairs)
+
+    copy = remote(last, sibling_last, sends.at[0], receives.at[0], {"ctx": sibling})
+    copy.start()
+    copy.wait()
+    mine, theirs = last[side], sibling_last[side]
+    leap = jump[side]
+    late = side == (1 if forward else 0)
+    farther = jnp.where(late, theirs, mine)
+    nearer = jnp.where(late, mine, theirs)
+    moved = turn(leap, farther, modes)
+    joined = [moved[0] + nearer[:modes], moved[1] + nearer[modes : 2 * modes]]
+    if last.shape[1] > 2 * modes:
+        joined.append(mine[2 * modes :] + theirs[2 * modes :])
+    slots[pair] = jnp.concatenate(joined, axis=0).astype(slots.dtype)
+
+    copies = []
+    for off in range(1, pairs):
+        to = lax.rem(pair + off, pairs) * 2 + side
+        copies.append(
+            remote(slots.at[pair], slots.at[pair], sends.at[off], receives.at[off], {"ctx": to})
+        )
+    for copy in copies:
+        copy.start()
+    for copy in copies:
+        copy.wait()
+    twice = jnp.concatenate(product((leap[:modes], leap[modes:]), (leap[:modes], leap[modes:])))
+    total = jnp.zeros((2 * modes, leap.shape[1]), F32)
+    for p in range(pairs) if forward else reversed(range(pairs)):
+        state = slots[p].astype(F32)
+        moved = jnp.concatenate(turn(twice, total, modes), axis=0) + state[: 2 * modes]
+        total = jnp.where(p < pair if forward else p > pair, moved, total)
+    own[0 : 2 * modes, :] = total
+    if last.shape[1] > 2 * modes:
+        rest = slots[0, 2 * modes :, :].astype(F32)
+        for p in range(1, pairs):
+            rest = rest + slots[p, 2 * modes :, :].astype(F32)
+        own[2 * modes :, :] = rest
+
+    copy = remote(own, other, sends.at[pairs], receives.at[pairs], {"ctx": sibling})
+    copy.start()
+    copy.wait()
+    for half in range(2):
+        state = jnp.where(side == half, own[...], other[...])
+        moved = jnp.concatenate(turn(jump[half], state, modes), axis=0)
+        moved = moved + sibling_last[half, 0 : 2 * modes, :]
+        first[half, 0 : 2 * modes, :] = jnp.where(late, moved, state[: 2 * modes])
+        if last.shape[1] > 2 * modes:
+            first[half, 2 * modes :, :] = state[2 * modes :]
+
+
+def norm_kernel(peers, squares, inners, scale_wide, inner_wide, slots, sends, receives):
+    me = lax.axis_index("tp")
+    barrier = pltpu.get_barrier_semaphore()
+    for off in range(1, peers):
+        pl.semaphore_signal(
+            barrier,
+            inc=1,
+            device_id={"tp": lax.rem(me + off, peers)},
+            device_id_type=pl.DeviceIdType.MESH,
+        )
+    tokens = squares.shape[0]
+    square_row = jnp.sum(squares[...].T, axis=0, keepdims=True)
+    inner_row = jnp.sum(inners[...].T, axis=0, keepdims=True)
+    upper = lax.broadcasted_iota(jnp.int32, (8, tokens), 0) < 4
+    slots[me] = jnp.where(upper, square_row, inner_row)
+    pl.semaphore_wait(barrier, peers - 1)
+    copies = [
+        remote(
+            slots.at[me],
+            slots.at[me],
+            sends.at[off - 1],
+            receives.at[off - 1],
+            {"tp": lax.rem(me + off, peers)},
+        )
+        for off in range(1, peers)
+    ]
+    for copy in copies:
+        copy.start()
+    for copy in copies:
+        copy.wait()
+    total = slots[0]
+    for p in range(1, peers):
+        total = total + slots[p]
+    scale = lax.rsqrt(total[0:1] / D + EPS)
+    inner = total[4:5] * scale / D
+    scale_wide[...] = jnp.broadcast_to(scale, (LANES, tokens)).T
+    inner_wide[...] = jnp.broadcast_to(inner, (LANES, tokens)).T
 
 
 def body(query, key, value, up, rates, freqs, residues, passthrough, norm_gain):
@@ -259,24 +381,38 @@
     chunks = tokens // (B * SEGMENTS)
     blocks = width // LANES
     groups = lax.axis_size("ctx")
-    me = lax.axis_index("ctx")
     size = jnp.exp(-rates)
     root = jnp.stack([size * jnp.cos(freqs), size * jnp.sin(freqs)])
     weight = residues * jnp.sqrt(rates)
     skip = passthrough[None, :]
     gain = norm_gain[None, :]
 
-    def first_state(every, order):
-        away = jnp.where(order > 0, order - 1, 0)[:, None, None].astype(F32) * tokens
-        on = (order > 0)[:, None, None]
-        size = jnp.where(on, jnp.exp(-rates[None] * away), 0.0)
-        re, im = size * jnp.cos(freqs[None] * away), size * jnp.sin(freqs[None] * away)
-        s_re, s_im = every[:, :modes], every[:, modes : 2 * modes]
-        return jnp.stack(
-            [jnp.sum(re * s_re - im * s_im, axis=0), jnp.sum(re * s_im + im * s_re, axis=0)]
-        )
-
-    place = jnp.arange(groups)
+    half = width // 2
+    turns = freqs * tokens
+    size = jnp.exp(-rates * tokens)
+    jump = jnp.concatenate([size * jnp.cos(turns), size * jnp.sin(turns)])
+    jump = jump.reshape(2 * modes, 2, half).transpose(1, 0, 2)
+
+    def exchange(last, forward):
+        rows = last.shape[1]
+        pairs = groups // 2
+        return pl.pallas_call(
+            functools.partial(exchange_kernel, modes, groups, forward),
+            in_specs=[pl.BlockSpec(memory_space=pltpu.VMEM)] * 2,
+            out_specs=pl.BlockSpec(memory_space=pltpu.VMEM),
+            out_shape=jax.ShapeDtypeStruct((2, rows, half), F32),
+            scratch_shapes=[
+                pltpu.VMEM((2, rows, half), F32),
+                pltpu.VMEM((pairs, rows, half), BF16),
+                pltpu.VMEM((rows, half), F32),
+                pltpu.VMEM((rows, half), F32),
+                pltpu.SemaphoreType.DMA((pairs + 1,)),
+                pltpu.SemaphoreType.DMA((pairs + 1,)),
+            ],
+            compiler_params=pltpu.CompilerParams(
+                collective_id=0 if forward else 1, has_side_effects=True
+            ),
+        )(last, jump)
 
     def columns(*rows):
         return pl.BlockSpec(rows + (LANES,), lambda i: (0,) * len(rows) + (i,))
@@ -285,6 +421,11 @@
     fixed = pl.BlockSpec((tokens, LANES), lambda i: (0, 0))
     row = columns(1)
     pair = columns(2, modes)
+
+    def halved(rows):
+        per = blocks // 2
+        return pl.BlockSpec((1, rows, LANES), lambda i: (i // per, 0, i % per))
+
     mode = columns(modes)
     states_spec = columns(2 * modes * chunks * SEGMENTS)
     ends_spec = columns(2 * modes * SEGMENTS)
@@ -322,39 +463,47 @@
     states, ends, last = call(
         forward_states_kernel,
         [tile, tile, pair],
-        [states_spec, ends_spec, columns(2 * modes)],
-        [states_shape, ends_shape, wide(2 * modes)],
+        [states_spec, ends_spec, halved(2 * modes)],
+        [states_shape, ends_shape, jax.ShapeDtypeStruct((2, 2 * modes, half), F32)],
         [],
         key, value, root,
     )
-    first = first_state(lax.all_gather(last, "ctx", axis=0), me - place)
+    first = exchange(last, True)
     conv, squares, inners = call(
         forward_kernel,
-        [tile, tile, tile, tile, row, states_spec, ends_spec, pair, pair, mode, row],
+        [tile, tile, tile, tile, row, states_spec, ends_spec, halved(2 * modes), pair, mode, row],
         [tile, fixed, fixed],
         [field_shape, sums_shape, sums_shape],
         more,
         key, value, query, up, gain, states, ends, first, root, weight, skip,
     )
-    sums = lax.psum(jnp.stack([jnp.sum(squares, axis=1), jnp.sum(inners, axis=1)]), "tp")
-    scale = lax.rsqrt(sums[0] / D + EPS)
-    inner = sums[1] * scale / D
-    scale_wide = jnp.broadcast_to(scale[:, None], (tokens, LANES))
-    inner_wide = jnp.broadcast_to(inner[:, None], (tokens, LANES))
+    peers = lax.axis_size("tp")
+    scale_wide, inner_wide = pl.pallas_call(
+        functools.partial(norm_kernel, peers),
+        in_specs=[pl.BlockSpec(memory_space=pltpu.VMEM)] * 2,
+        out_specs=[pl.BlockSpec(memory_space=pltpu.VMEM)] * 2,
+        out_shape=[sums_shape] * 2,
+        scratch_shapes=[
+            pltpu.VMEM((peers, 8, tokens), F32),
+            pltpu.SemaphoreType.DMA((peers - 1,)),
+            pltpu.SemaphoreType.DMA((peers - 1,)),
+        ],
+        compiler_params=pltpu.CompilerParams(collective_id=2, has_side_effects=True),
+    )(squares, inners)
     output, query_grad, conv_grad, states, ends, last = call(
         middle_kernel,
         [tile, tile, tile, row, fixed, fixed, pair],
-        [tile, tile, tile, states_spec, ends_spec, columns(2 * modes + 8)],
-        [field_shape] * 3 + [states_shape, ends_shape, wide(2 * modes + 8)],
+        [tile, tile, tile, states_spec, ends_spec, halved(2 * modes + 16)],
+        [field_shape] * 3
+        + [states_shape, ends_shape, jax.ShapeDtypeStruct((2, 2 * modes + 16, half), F32)],
         [],
         query, up, conv, gain, scale_wide, inner_wide, root,
     )
-    every = lax.all_gather(last[: 2 * modes + 1], "ctx", axis=0)
-    gain_grad = jnp.sum(every[:, 2 * modes], axis=0)
-    first = first_state(every, place - me)
+    first = exchange(last, False)
+    gain_grad = first[:, 2 * modes].reshape(width)
     key_grad, value_grad = call(
         backward_kernel,
-        [tile, tile, tile, states_spec, ends_spec, pair, pair, mode, row],
+        [tile, tile, tile, states_spec, ends_spec, halved(2 * modes + 16), pair, mode, row],
         [tile, tile],
         [field_shape] * 2,
         more,

time: 169 us -> 117 us (0.69)
  waiting for transfers between devices: 46.3 us -> 0 us
  Pallas kernels: 78.7 us -> 112 us
  between operations: 14.1 us -> 0.67 us
  other arithmetic: 15.5 us -> 2.67 us
  blocking collectives: 9.99 us -> 0 us
    all_gather x2 -> x0, waiting for transfers between devices: 46.3 us -> none  [the longest x1 24.9 us: body(): first = first_state(lax.all_gather(last, 'ctx', axis=0), me - place)]
    pallas_call x0 -> x3, Pallas kernels: none -> 32.5 us  [the longest x2 24.7 us: exchange(): pl.pallas_call(functools.partial(exchange_kernel, modes, groups, forward)...]
    reduce_sum x5 -> x0, other arithmetic: 11.7 us -> none  [the longest x2 7.6 us: first_state(): jnp.sum(re * s_re - im * s_im, axis=0)]
    psum x1 -> x0, blocking collectives: 9.99 us -> none  [body(): lax.psum(jnp.stack([jnp.sum(squares, axis=1), jnp.sum(inners, axis=1)]),...]
    broadcast_in_dim x2 -> x0, local copies, waits for them, and re-layouts: 2.02 us -> none  [the longest x1 1.03 us: body(): inner_wide = jnp.broadcast_to(inner[:, None], (tokens, LANES))]
    mul x2 -> x1, other arithmetic: 0.01 us -> 2.01 us  [body(): jump = jnp.concatenate([size * jnp.cos(turns), size * jnp.sin(turns)])]
    another operation x2 -> x1, other arithmetic: 2.41 us -> 0.65 us  [body(): root = jnp.stack([size * jnp.cos(freqs), size * jnp.sin(freqs)])]
  transfers between devices with their start and end apart: 2 -> 0, of which waited for: 2 -> 0; matrix products, arithmetic and copies ran while one was open for 0% -> 0% of each run, Pallas kernels for 0% -> 0%
where the time goes in v2:
time: 117 us
  Pallas kernels  112 us (96%)
  other arithmetic  2.67 us (2%)
  local copies, waits for them, and re-layouts  2.01 us (2%)
    pallas_call x4, Pallas kernels, call(): pl.pallas_call(functools.partial(kernel, modes, chunks), grid=(blocks,),...  79.2 us
    pallas_call x2, Pallas kernels, exchange(): pl.pallas_call(functools.partial(exchange_kernel, modes, groups, forward)...  24.7 us
    pallas_call x1, Pallas kernels, body(): pl.pallas_call(functools.partial(norm_kernel, peers), in_specs=[pl.BlockS...  7.81 us

profile of v2, /device:TPU:0, one launch (start us, length us, event | category | flops | bytes accessed | tf_op | source)
XLA Modules:
  0.0 117.0 jit_solution(14982806378915144549)
XLA Ops:
  0.6 2.0 %cosine_multiply_fusion = (f32[16,1024]{1,0:T(8,128)S(1)}, f32[16,1024]{1,0:T(8,128)S(1)}, f32[1,16,1024]{2,1,0:T(8,128)S(1)}, f32[1,16,1024]{2,1,0:T(8,128)S(1)}, f32[16,1024]{1,0:T(8,128)}) fusion(f32[16,1024]{1,0:T(8,128)} %param.14, f32[16,1024]{1,0:T(8,128)} %param.13, f32[16,1024]{1,0:T(8,128)} %param.15), kind=kLoop, calls=%fused_computation.5 | loop fusion | flops 131072 | bytes 524288 | tf_op jit(solution)/shard_map/mul | solution.py:393
  2.7 0.7 copy.17
  3.3 0.7 pad_maximum_fusion.root
  4.0 16.1 %shard_map.128 = (f32[2048,1024]{1,0:T(8,128)}, f32[256,1024]{1,0:T(8,128)}, f32[2,32,512]{2,1,0:T(8,128)}) custom-call(bf16[1024,1024]{1,0:T(8,128)(2,1)} %key.5, bf16[1024,1024]{1,0:T(8,128)(2,1)} %value.5, f32[2,16,1024]{2,1,0:T(8,128)} %pad_maximum_fusion.root), custom_call_target="tpu_custom_call" | custom-call | tf_op jit(solution)/shard_map/pallas_call | solution.py:453
  20.1 12.5 %shard_map.129.first = f32[2,32,512]{2,1,0:T(8,128)} custom-call(f32[2,32,512]{2,1,0:T(8,128)} %get-tuple-element.23.last, f32[2,32,512]{2,1,0:T(8,128)} %bitcast.14), custom_call_target="tpu_custom_call" | custom-call | tf_op jit(solution)/shard_map/pallas_call | solution.py:399
  32.6 21.9 %shard_map.130 = (bf16[1024,1024]{1,0:T(8,128)(2,1)}, f32[1024,128]{1,0:T(8,128)}, f32[1024,128]{1,0:T(8,128)}) custom-call(bf16[1024,1024]{1,0:T(8,128)(2,1)} %key.5, bf16[1024,1024]{1,0:T(8,128)(2,1)} %value.5, bf16[1024,1024]{1,0:T(8,128)(2,1)} %query.3, bf16[1024,1024]{1,0:T(8,128)(2,1)} %up.3, f32[1,1024]{1,0:T(1,128)} %bitcast.17, ...), custom_call_target="tpu_custom_call" | custom-call | tf_op jit(solution)/shard_map/pallas_call | solution.py:453
  54.5 7.8 %shard_map.131 = (f32[1024,128]{1,0:T(8,128)}, f32[1024,128]{1,0:T(8,128)}) custom-call(f32[1024,128]{1,0:T(8,128)} %get-tuple-element.25.squares, f32[1024,128]{1,0:T(8,128)} %get-tuple-element.26.inners), custom_call_target="tpu_custom_call" | custom-call | tf_op jit(solution)/shard_map/pallas_call | solution.py:481
  62.3 20.9 %shard_map.132 = (bf16[1024,1024]{1,0:T(8,128)(2,1)}, bf16[1024,1024]{1,0:T(8,128)(2,1)}, bf16[1024,1024]{1,0:T(8,128)(2,1)}, f32[2048,1024]{1,0:T(8,128)}, f32[256,1024]{1,0:T(8,128)}, /*index=5*/f32[2,48,512]{2,1,0:T(8,128)}) custom-call(bf16[1024,1024]{1,0:T(8,128)(2,1)} %query.3, bf16[1024,1024]{1,0:T(8,128)(2,1)} %up.3, ...), custom_call_target="tpu_custom_call" | custom-call | tf_op jit(solution)/shard_map/pallas_call | solution.py:453
  83.2 12.1 %shard_map.133.first = f32[2,48,512]{2,1,0:T(8,128)} custom-call(f32[2,48,512]{2,1,0:T(8,128)} %get-tuple-element.34.last, f32[2,32,512]{2,1,0:T(8,128)} %bitcast.15), custom_call_target="tpu_custom_call" | custom-call | tf_op jit(solution)/shard_map/pallas_call | solution.py:399
  95.4 20.3 %shard_map.134 = (bf16[1024,1024]{1,0:T(8,128)(2,1)}, bf16[1024,1024]{1,0:T(8,128)(2,1)}) custom-call(bf16[1024,1024]{1,0:T(8,128)(2,1)} %get-tuple-element.31.conv_grad, bf16[1024,1024]{1,0:T(8,128)(2,1)} %key.5, bf16[1024,1024]{1,0:T(8,128)(2,1)} %value.5, f32[2048,1024]{1,0:T(8,128)} %get-tuple-element.32.states, f32[256,1024]{1,0:T(8,128)} %get-tuple-element.33.ends, ...), custom_call_target="tpu_custom_call" | custom-call | tf_op jit(solution)/shard_map/pallas_call | solution.py:453
  115.6 1.4 %slice.3 = f32[2,1,512]{2,1,0:T(1,128)} slice(f32[2,48,512]{2,1,0:T(8,128)} %shard_map.133.first), slice={[0:2], [32:33], [0:512]} | slice | bytes 8192 | tf_op jit(solution)/shard_map/slice | solution.py:503
  (1 shorter events, 0.0 us)

commit v3 on v2

--- a/solution.py
+++ b/solution.py
@@ -177,7 +177,7 @@
 
 
 def forward_states_kernel(
-    modes, chunks, key, value, root, states, ends, last, nat, perm, powers
+    modes, chunks, key, value, root, states, ends, last, perm, nat, powers
 ):
     far = build_powers(root, powers, chunks)
     field = (key[...].astype(F32) * value[...].astype(F32)).astype(BF16).astype(F32)
@@ -190,13 +190,11 @@
 
 
 def forward_kernel(
-    modes, chunks, key, value, query, up, gain, states, ends, first, root, weight, skip,
-    conv, squares, inners, nat, perm, powers, incoming, taps, starts,
+    modes, chunks, perm, query, up, gain, states, ends, first, root, weight, skip,
+    conv, squares, inners, nat, powers, incoming, taps, starts,
 ):
     far = build_powers(root, powers, chunks)
     build_taps(powers, weight, skip, taps)
-    field = (key[...].astype(F32) * value[...].astype(F32)).astype(BF16).astype(F32)
-    token_rows(field, nat, perm, chunks)
     scan_segments(ends, (first[0, 0:modes, :], first[0, modes : 2 * modes, :]), far, starts, modes, True)
     scan_chunks(states, starts, powers, weight, incoming, modes, chunks, True)
     expand(perm, incoming, taps, powers, nat, modes, chunks, True)
@@ -215,7 +213,7 @@
 
 def middle_kernel(
     modes, chunks, query, up, conv, gain, scale, inner, root,
-    output, query_grad, conv_grad, states, ends, last, nat, perm, powers,
+    output, query_grad, states, ends, last, perm, nat, powers,
 ):
     q = query[...].astype(F32)
     c = conv[...].astype(F32)
@@ -227,7 +225,6 @@
     grad_gated = s * (u * gain[...] - normed * inner[...])
     query_grad[...] = (grad_gated * c).astype(BF16)
     w = (grad_gated * q).astype(BF16)
-    conv_grad[...] = w
     far = build_powers(root, powers, chunks)
     token_rows(w.astype(F32), nat, perm, chunks)
     chunk_states(perm, powers, states, ends, modes, chunks, False)
@@ -239,12 +236,11 @@
 
 
 def backward_kernel(
-    modes, chunks, conv_grad, key, value, states, ends, first, root, weight, skip,
-    key_grad, value_grad, nat, perm, powers, incoming, taps, starts,
+    modes, chunks, perm, key, value, states, ends, first, root, weight, skip,
+    key_grad, value_grad, nat, powers, incoming, taps, starts,
 ):
     far = build_powers(root, powers, chunks)
     build_taps(powers, weight, skip, taps)
-    token_rows(conv_grad[...].astype(F32), nat, perm, chunks)
     scan_segments(ends, (first[0, 0:modes, :], first[0, modes : 2 * modes, :]), far, starts, modes, False)
     scan_chunks(states, starts, powers, weight, incoming, modes, chunks, False)
     expand(perm, incoming, taps, powers, nat, modes, chunks, False)
@@ -439,7 +435,6 @@
     ends_shape = wide(2 * modes * SEGMENTS)
     scratch = [
         pltpu.VMEM((tokens + 8 * SEGMENTS, LANES), F32),
-        pltpu.VMEM((tokens, LANES), F32),
         pltpu.VMEM((2 * (B + 1), modes, LANES), F32),
     ]
     more = [
@@ -460,22 +455,22 @@
             compiler_params=params,
         )(*args)
 
-    states, ends, last = call(
+    states, ends, last, perm = call(
         forward_states_kernel,
         [tile, tile, pair],
-        [states_spec, ends_spec, halved(2 * modes)],
-        [states_shape, ends_shape, jax.ShapeDtypeStruct((2, 2 * modes, half), F32)],
+        [states_spec, ends_spec, halved(2 * modes), tile],
+        [states_shape, ends_shape, jax.ShapeDtypeStruct((2, 2 * modes, half), F32), wide(tokens)],
         [],
         key, value, root,
     )
     first = exchange(last, True)
     conv, squares, inners = call(
         forward_kernel,
-        [tile, tile, tile, tile, row, states_spec, ends_spec, halved(2 * modes), pair, mode, row],
+        [tile, tile, tile, row, states_spec, ends_spec, halved(2 * modes), pair, mode, row],
         [tile, fixed, fixed],
         [field_shape, sums_shape, sums_shape],
         more,
-        key, value, query, up, gain, states, ends, first, root, weight, skip,
+        perm, query, up, gain, states, ends, first, root, weight, skip,
     )
     peers = lax.axis_size("tp")
     scale_wide, inner_wide = pl.pallas_call(
@@ -490,12 +485,13 @@
         ],
         compiler_params=pltpu.CompilerParams(collective_id=2, has_side_effects=True),
     )(squares, inners)
-    output, query_grad, conv_grad, states, ends, last = call(
+    output, query_grad, states, ends, last, perm = call(
         middle_kernel,
         [tile, tile, tile, row, fixed, fixed, pair],
-        [tile, tile, tile, states_spec, ends_spec, halved(2 * modes + 16)],
-        [field_shape] * 3
-        + [states_shape, ends_shape, jax.ShapeDtypeStruct((2, 2 * modes + 16, half), F32)],
+        [tile, tile, states_spec, ends_spec, halved(2 * modes + 16), tile],
+        [field_shape] * 2
+        + [states_shape, ends_shape, jax.ShapeDtypeStruct((2, 2 * modes + 16, half), F32)]
+        + [wide(tokens)],
         [],
         query, up, conv, gain, scale_wide, inner_wide, root,
     )
@@ -507,7 +503,7 @@
         [tile, tile],
         [field_shape] * 2,
         more,
-        conv_grad, key, value, states, ends, first, root, weight, skip,
+        perm, key, value, states, ends, first, root, weight, skip,
     )
     return output, query_grad, key_grad, value_grad, gain_grad
 

time: 117 us -> 115 us (0.983)
  Pallas kernels: 112 us -> 110 us
    pallas_call x4, Pallas kernels: 79.2 us -> 77.1 us  [call(): pl.pallas_call(functools.partial(kernel, modes, chunks), grid=(blocks,),...]
where the time goes in v3:
time: 115 us
  Pallas kernels  110 us (96%)
  other arithmetic  2.68 us (2%)
  local copies, waits for them, and re-layouts  2.01 us (2%)
    pallas_call x4, Pallas kernels, call(): pl.pallas_call(functools.partial(kernel, modes, chunks), grid=(blocks,),...  77.1 us
    pallas_call x2, Pallas kernels, exchange(): pl.pallas_call(functools.partial(exchange_kernel, modes, groups, forward)...  24.7 us
    pallas_call x1, Pallas kernels, body(): pl.pallas_call(functools.partial(norm_kernel, peers), in_specs=[pl.BlockS...  7.8 us

profile of v3, /device:TPU:0, one launch (start us, length us, event | category | flops | bytes accessed | tf_op | source)
XLA Modules:
  0.0 114.9 jit_solution(2503478150101686402)
XLA Ops:
  0.6 2.0 %cosine_multiply_fusion = (f32[16,1024]{1,0:T(8,128)S(1)}, f32[16,1024]{1,0:T(8,128)S(1)}, f32[1,16,1024]{2,1,0:T(8,128)S(1)}, f32[1,16,1024]{2,1,0:T(8,128)S(1)}, f32[16,1024]{1,0:T(8,128)}) fusion(f32[16,1024]{1,0:T(8,128)} %param.14, f32[16,1024]{1,0:T(8,128)} %param.13, f32[16,1024]{1,0:T(8,128)} %param.15), kind=kLoop, calls=%fused_computation.5 | loop fusion | flops 131072 | bytes 524288 | tf_op jit(solution)/shard_map/mul | solution.py:389
  2.7 0.7 copy.17
  3.3 0.7 pad_maximum_fusion.root
  4.0 16.3 %shard_map.128 = (f32[2048,1024]{1,0:T(8,128)}, f32[256,1024]{1,0:T(8,128)}, f32[2,32,512]{2,1,0:T(8,128)}, f32[1024,1024]{1,0:T(8,128)}) custom-call(bf16[1024,1024]{1,0:T(8,128)(2,1)} %key.3, bf16[1024,1024]{1,0:T(8,128)(2,1)} %value.3, f32[2,16,1024]{2,1,0:T(8,128)} %pad_maximum_fusion.root), custom_call_target="tpu_custom_call" | custom-call | tf_op jit(solution)/shard_map/pallas_call | solution.py:448
  20.2 12.5 %shard_map.129.first = f32[2,32,512]{2,1,0:T(8,128)} custom-call(f32[2,32,512]{2,1,0:T(8,128)} %get-tuple-element.25.last, f32[2,32,512]{2,1,0:T(8,128)} %bitcast.14), custom_call_target="tpu_custom_call" | custom-call | tf_op jit(solution)/shard_map/pallas_call | solution.py:395
  32.8 20.2 %shard_map.130 = (bf16[1024,1024]{1,0:T(8,128)(2,1)}, f32[1024,128]{1,0:T(8,128)}, f32[1024,128]{1,0:T(8,128)}) custom-call(f32[1024,1024]{1,0:T(8,128)} %get-tuple-element.22.perm, bf16[1024,1024]{1,0:T(8,128)(2,1)} %query.3, bf16[1024,1024]{1,0:T(8,128)(2,1)} %up.3, f32[1,1024]{1,0:T(1,128)} %bitcast.17, f32[2048,1024]{1,0:T(8,128)} %get-tuple-element.23.states, ...), custom_call_target="tpu_custom_call" | custom-call | tf_op jit(solution)/shard_map/pallas_call | solution.py:448
  52.9 7.8 %shard_map.131 = (f32[1024,128]{1,0:T(8,128)}, f32[1024,128]{1,0:T(8,128)}) custom-call(f32[1024,128]{1,0:T(8,128)} %get-tuple-element.27.squares, f32[1024,128]{1,0:T(8,128)} %get-tuple-element.28.inners), custom_call_target="tpu_custom_call" | custom-call | tf_op jit(solution)/shard_map/pallas_call | solution.py:476
  60.8 21.2 %shard_map.132 = (bf16[1024,1024]{1,0:T(8,128)(2,1)}, bf16[1024,1024]{1,0:T(8,128)(2,1)}, f32[2048,1024]{1,0:T(8,128)}, f32[256,1024]{1,0:T(8,128)}, f32[2,48,512]{2,1,0:T(8,128)}, /*index=5*/f32[1024,1024]{1,0:T(8,128)}) custom-call(bf16[1024,1024]{1,0:T(8,128)(2,1)} %query.3, bf16[1024,1024]{1,0:T(8,128)(2,1)} %up.3, ...), custom_call_target="tpu_custom_call" | custom-call | tf_op jit(solution)/shard_map/pallas_call | solution.py:448
  81.9 12.1 %shard_map.133.first = f32[2,48,512]{2,1,0:T(8,128)} custom-call(f32[2,48,512]{2,1,0:T(8,128)} %get-tuple-element.36.last, f32[2,32,512]{2,1,0:T(8,128)} %bitcast.15), custom_call_target="tpu_custom_call" | custom-call | tf_op jit(solution)/shard_map/pallas_call | solution.py:395
  94.1 19.5 %shard_map.134 = (bf16[1024,1024]{1,0:T(8,128)(2,1)}, bf16[1024,1024]{1,0:T(8,128)(2,1)}) custom-call(f32[1024,1024]{1,0:T(8,128)} %get-tuple-element.33.perm, bf16[1024,1024]{1,0:T(8,128)(2,1)} %key.3, bf16[1024,1024]{1,0:T(8,128)(2,1)} %value.3, f32[2048,1024]{1,0:T(8,128)} %get-tuple-element.34.states, f32[256,1024]{1,0:T(8,128)} %get-tuple-element.35.ends, ...), custom_call_target="tpu_custom_call" | custom-call | tf_op jit(solution)/shard_map/pallas_call | solution.py:448
  113.6 1.4 %slice.3 = f32[2,1,512]{2,1,0:T(1,128)} slice(f32[2,48,512]{2,1,0:T(8,128)} %shard_map.133.first), slice={[0:2], [32:33], [0:512]} | slice | bytes 8192 | tf_op jit(solution)/shard_map/slice | solution.py:499
  (1 shorter events, 0.0 us)
